TPU v7x, 128 devices: a whole 4x4x4 slice. The times are simulated.
128 devices in a mesh: group: 8 (over z, core), lane: 16 (over y, x).
Axes of the slice: x: 4, y: 4, z: 4, core: 2. Of those that a mesh axis runs over, the one named last changes fastest.
Arguments:
- tokens: bfloat16 [2048, 7168], P(('group', 'lane')), may hold values from -6 to 6
- expert_ids: int32 [2048, 8], P(('group', 'lane')), may hold values from 0 to 31, as said below
- gate_weights: float32 [2048, 8], P(('group', 'lane')), may hold values from 0.05 to 0.6
- w_gate: bfloat16 [128, 7168, 512], P(('group', 'lane')), may hold values from -0.0625 to 0.0625
- w_up: bfloat16 [128, 7168, 512], P(('group', 'lane')), may hold values from -0.0625 to 0.0625
- w_down: bfloat16 [128, 2048, 1792], P(('group', 'lane')), may hold values from -0.125 to 0.125
Outputs:
- moe_output: bfloat16 [2048, 7168], P(('group', 'lane'))
Inputs may be any that keep to these rules, and one draw needn't show every extreme that they name: `expert_ids`: each row names 8 different experts that lie in at most 4 groups, expert e being in group e // 4. Among the 16 rows of one device no expert is named by more than 8 rows, and in every draw one expert is named by exactly 8 rows of every device.
All inputs are finite; a program needn't handle non-finite values.
Results may differ from a plain program's by a relative error of at most 0.012.
Values may be sent and summed in bfloat16 or wider, within the bound.
A program may use at most 128 MiB of HBM per device.

v0:
```python
import jax
import jax.numpy as jnp
from jax import lax
from jax.sharding import PartitionSpec as P

TOPK = 8
HSPLIT = 4


def from_partner(array, axis, distance):
    return lax.ppermute(array, axis, [(i, i ^ 1 << distance) for i in range(lax.axis_size(axis))])


def per_device(tokens, expert_ids, gate_weights, w_gate, w_up, w_down):
    groups = lax.axis_size("group")
    lane_count = lax.axis_size("lane")
    experts = groups * lane_count // HSPLIT
    tok_rows = tokens.shape[0]
    model_width = tokens.shape[1]
    out_cols = w_down.shape[2]
    capacity = min(tok_rows, 2 * tok_rows * TOPK // experts)
    expert_range = jnp.arange(experts, dtype=jnp.int32)
    picked = (expert_ids[:, :, None] == expert_range[None, None, :]).astype(jnp.int32)
    named_count = jnp.sum(picked, axis=1)
    before = jnp.cumsum(named_count, axis=0) - named_count
    slot_of = jnp.sum(picked * before[:, None, :], axis=2)
    target = expert_ids * capacity + slot_of
    slot_all = jnp.arange(experts * capacity, dtype=jnp.int32)
    placing = jnp.any(slot_all[:, None, None] == target[None, :, :], axis=2).astype(jnp.bfloat16)
    outgoing = jnp.dot(placing, tokens, preferred_element_type=jnp.float32).astype(jnp.bfloat16)
    outgoing = outgoing.reshape(experts, capacity, model_width)
    copies = jnp.repeat(outgoing, HSPLIT, axis=0)
    received = lax.all_to_all(copies, ("group", "lane"), split_axis=0, concat_axis=0, tiled=True)
    expert_rows = received.reshape(groups * lane_count * capacity, model_width)
    gate_values = jnp.dot(expert_rows, w_gate[0], preferred_element_type=jnp.float32)
    up_values = jnp.dot(expert_rows, w_up[0], preferred_element_type=jnp.float32)
    hidden = (jax.nn.silu(gate_values) * up_values).astype(jnp.bfloat16)
    lane_index = lax.axis_index("lane")
    joined = hidden
    for doubling in range(HSPLIT.bit_length() - 1):
        partner = from_partner(joined, "lane", doubling)
        lower_half = lane_index // 2**doubling % 2 == 0
        joined = jnp.where(
            lower_half,
            jnp.concatenate([joined, partner], axis=1),
            jnp.concatenate([partner, joined], axis=1),
        )
    expert_out = jnp.dot(joined, w_down[0], preferred_element_type=jnp.float32).astype(jnp.bfloat16)
    expert_out = expert_out.reshape(groups, lane_count, capacity, out_cols)
    returned = lax.all_to_all(
        expert_out.reshape(groups * lane_count, capacity, out_cols),
        ("group", "lane"),
        split_axis=0,
        concat_axis=0,
        tiled=True,
    )
    column_blocks = returned.reshape(experts, HSPLIT, capacity, out_cols)
    gathered = column_blocks[expert_ids, :, slot_of, :]
    mixed = jnp.einsum("tk,tksc->tsc", gate_weights, gathered.astype(jnp.float32))
    return mixed.reshape(tok_rows, model_width).astype(jnp.bfloat16)


def solution(mesh):
    in_specs = (
        P(("group", "lane"), None),
        P(("group", "lane"), None),
        P(("group", "lane"), None),
        P(("group", "lane"), None, None),
        P(("group", "lane"), None, None),
        P(("group", "lane"), None, None),
    )
    out_specs = P(("group", "lane"), None)
    return jax.shard_map(
        per_device, mesh=mesh, in_specs=in_specs, out_specs=out_specs, check_vma=False
    )
```

profile of v0, /device:TPU:1, one launch (start us, length us, event | category | flops | bytes accessed | tf_op | source)
XLA Modules:
  0.0 360.3 jit_solution(8952392226738005685)
XLA Ops:
  0.0 0.0 copy-start
  0.0 0.8 copy.17
  0.8 0.1 convert_reduce_fusion
  0.9 0.4 select_reduce_fusion
  1.4 0.1 fusion.27
  1.5 0.0 copy-done
  1.5 1.1 fusion.4
  2.7 2.0 broadcast_in_dim.4
  4.6 175.9 %all_to_all.10 = bf16[128,8,7168]{2,1,0:T(8,128)(2,1)} all-to-all(bf16[128,8,7168]{2,1,0:T(8,128)(2,1)S(1)} %bitcast.46), channel_id=1, replica_groups=mesh['group'=8,'lane'=16] {'group','lane'}, dimensions={0} | all-to-all | bytes 29360128 | tf_op jit(solution)/shard_map/all_to_all | solution.py:33
  180.6 13.2 %fusion = f32[1024,512]{0,1:T(8,128)S(1)} fusion(bf16[128,8,7168]{2,1,0:T(8,128)(2,1)} %all_to_all.10, bf16[1,7168,512]{2,1,0:T(8,128)(2,1)} %param.10), kind=kOutput, calls=%fused_computation.1 | convolution fusion | flops 7516192768 | bytes 24117248 | tf_op jit(solution)/shard_map/dot_general | solution.py:36
  193.8 13.5 %multiply_convert_fusion = bf16[1024,512]{0,1:T(8,128)(2,1)S(1)} fusion(f32[1024,512]{0,1:T(8,128)S(1)} %fusion, bf16[1,7168,512]{2,1,0:T(8,128)(2,1)} %param.9, bf16[128,8,7168]{2,1,0:T(8,128)(2,1)} %all_to_all.10), kind=kOutput, calls=%fused_computation.21 | convolution fusion | flops 7519338496 | bytes 25165824 | tf_op jit(solution)/shard_map/dot_general | solution.py:35
  207.3 1.3 collective-permute-start
  208.5 22.5 %collective-permute-done = bf16[1024,512]{0,1:T(8,128)(2,1)} collective-permute-done((bf16[1024,512]{0,1:T(8,128)(2,1)S(1)}, bf16[1024,512]{0,1:T(8,128)(2,1)}, u32[]{:S(2)}, u32[]{:S(2)}) %collective-permute-start) | collective-permute-done | bytes 1048608 | tf_op jit(solution)/shard_map/ppermute | solution.py:11
  231.1 2.5 maximum_select_fusion.6
  233.6 3.3 collective-permute-start.1
  236.9 43.9 %collective-permute-done.1 = bf16[1024,1024]{0,1:T(8,128)(2,1)} collective-permute-done((bf16[1024,1024]{0,1:T(8,128)(2,1)S(1)}, bf16[1024,1024]{0,1:T(8,128)(2,1)}, u32[]{:S(2)}, u32[]{:S(2)}) %collective-permute-start.1) | collective-permute-done | bytes 2097184 | tf_op jit(solution)/shard_map/ppermute | solution.py:11
  280.8 13.3 %fusion.18 = bf16[128,8,1792]{2,1,0:T(8,128)(2,1)} fusion(bf16[1,2048,1792]{2,1,0:T(8,128)(2,1)} %param.11, bf16[1024,1024]{0,1:T(8,128)(2,1)} %collective-permute-done.1, bf16[1024,1024]{0,1:T(8,128)(2,1)S(1)} %maximum_select_fusion.6, pred[]{:T(512)S(6)} %eq.35), kind=kOutput, calls=%fused_computation.19 | convolution fusion | flops 7536902144 | bytes 15204353 | tf_op jit(solution)/shard_map/dot_general | solution.py:48
  294.2 0.0 copy-start.2
  294.2 0.0 copy-start.3
  294.2 8.6 %all-to-all-start.1 = ((bf16[128,8,1792]{2,1,0:T(8,128)(2,1)}), bf16[128,8,1792]{2,1,0:T(8,128)(2,1)}, u32[]{:S(2)}, u32[]{:S(2)}) async-start(bf16[128,8,1792]{2,1,0:T(8,128)(2,1)} %fusion.18), calls=%async_computation.1 | async-start | bytes 7340032 | tf_op jit(solution)/shard_map/all_to_all | solution.py:50
  302.7 0.1 copy.19
  302.8 0.0 copy-done.2
  302.8 0.1 copy.20
  302.9 0.1 reshape.42
  303.0 0.0 copy-done.3
  303.0 0.1 copy.23
  303.1 45.7 %all-to-all-done.1 = bf16[128,8,1792]{2,1,0:T(8,128)(2,1)} async-done(((bf16[128,8,1792]{2,1,0:T(8,128)(2,1)}), bf16[128,8,1792]{2,1,0:T(8,128)(2,1)}, u32[]{:S(2)}, u32[]{:S(2)}) %all-to-all-start.1) | async-done | bytes 3670048 | tf_op jit(solution)/shard_map/all_to_all | solution.py:50
  348.7 0.0 copy-start.1
  348.7 5.7 %copy.21 = bf16[32,4,8,1792]{3,1,2,0:T(4,128)(2,1)} copy(bf16[32,4,8,1792]{3,2,1,0:T(8,128)(2,1)} %bitcast.7) | data formatting | bytes 7340032 | tf_op jit(solution)/shard_map/reshape | solution.py:57
  354.5 4.3 %gather_fusion = bf16[128,4,1792]{2,1,0:T(4,128)(2,1)S(1)} fusion(bf16[32,4,8,1792]{3,1,2,0:T(4,128)(2,1)} %copy.21, s32[128]{0:T(128)S(1)} %reshape.42), kind=kCustom, calls=%fused_computation | custom fusion | bytes 3671040 | tf_op jit(solution)/shard_map/gather | solution.py:58
  358.8 0.6 fusion.25
  359.5 0.1 copy.29
  359.6 0.7 copy.25
  360.3 0.0 copy-done.1
  (4 shorter events, 0.1 us)
Async XLA Ops:
  0.0 1.5 copy-start
  207.3 23.8 %collective-permute-start = (bf16[1024,512]{0,1:T(8,128)(2,1)S(1)}, bf16[1024,512]{0,1:T(8,128)(2,1)}, u32[]{:S(2)}, u32[]{:S(2)}) collective-permute-start(bf16[1024,512]{0,1:T(8,128)(2,1)S(1)} %multiply_convert_fusion), channel_id=1, source_target_pairs={{0,1},{1,0},{2,3},{3,2},{4,5},{5,4},{6,7},{7,6},{8,9},{9,8},{10,11... | collective-permute-start | bytes 3145736 | tf_op jit(solution)/shard_map/ppermute | solution.py:11
  233.6 47.2 %collective-permute-start.1 = (bf16[1024,1024]{0,1:T(8,128)(2,1)S(1)}, bf16[1024,1024]{0,1:T(8,128)(2,1)}, u32[]{:S(2)}, u32[]{:S(2)}) collective-permute-start(bf16[1024,1024]{0,1:T(8,128)(2,1)S(1)} %maximum_select_fusion.6), channel_id=1, source_target_pairs={{0,2},{1,3},{2,0},{3,1},{4,6},{5,7},{6,4},{7,5},{8,10},{9,11},{10,... | collective-permute-start | bytes 6291464 | tf_op jit(solution)/shard_map/ppermute | solution.py:11
  294.2 8.7 %copy-start.2 = (s32[16,8]{0,1:T(8,128)S(1)}, s32[16,8]{0,1:T(8,128)}, u32[]{:S(2)}) copy-start(s32[16,8]{0,1:T(8,128)} %param.7) | copy-start | bytes 1540
  294.2 8.8 %copy-start.3 = (f32[16,8]{0,1:T(8,128)S(1)}, f32[16,8]{0,1:T(8,128)}, u32[]{:S(2)}) copy-start(f32[16,8]{0,1:T(8,128)} %param.8) | copy-start | bytes 1540
  294.2 54.6 %all-to-all-start.1 = ((bf16[128,8,1792]{2,1,0:T(8,128)(2,1)}), bf16[128,8,1792]{2,1,0:T(8,128)(2,1)}, u32[]{:S(2)}, u32[]{:S(2)}) async-start(bf16[128,8,1792]{2,1,0:T(8,128)(2,1)} %fusion.18), calls=%async_computation.1 | async-start | bytes 7340032 | tf_op jit(solution)/shard_map/all_to_all | solution.py:50
  348.7 11.6 %copy-start.1 = (bf16[16,7168]{1,0:T(8,128)(2,1)S(1)}, bf16[16,7168]{1,0:T(8,128)(2,1)}, u32[]{:S(2)}) copy-start(bf16[16,7168]{1,0:T(8,128)(2,1)} %param.6) | copy-start | bytes 688132
where the time goes:
time: 361 us; the launch traced here: 360 us
  blocking collectives  176 us (49%)
  waiting for transfers between devices  112 us (31%)
  matrix products  41.8 us (12%)
  local copies, waits for them, and re-layouts  14 us (4%)
  starting transfers between devices  13.1 us (4%)
    all_to_all x1, blocking collectives, per_device(): lax.all_to_all(copies, ('group', 'lane'), split_axis=0, concat_axis=0, ti...  176 us
    ppermute x2, waiting for transfers between devices, from_partner(): lax.ppermute(array, axis, [(i, i ^ 1 << distance) for i in range(lax.axis...  66.5 us
    all_to_all x1, waiting for transfers between devices, per_device(): lax.all_to_all(expert_out.reshape(groups * lane_count, capacity, out_cols...  45.7 us
    dot_general x1, matrix products, per_device(): jnp.dot(expert_rows, w_gate[0], preferred_element_type=jnp.float32)  13.5 us
    dot_general x1, matrix products, per_device(): jnp.dot(joined, w_down[0], preferred_element_type=jnp.float32)  13.3 us
    dot_general x1, matrix products, per_device(): jnp.dot(expert_rows, w_up[0], preferred_element_type=jnp.float32)  13.2 us
    all_to_all x1, starting transfers between devices, per_device(): lax.all_to_all(expert_out.reshape(groups * lane_count, capacity, out_cols...  8.57 us
  transfers between devices with their start and end apart: 3, of which 3 were waited for; matrix products, arithmetic and copies ran while one was open for 0% of the time, Pallas kernels for 0%

commit v1 on v0

v1 whole, which is shorter than its diff:
```python
import jax
import jax.numpy as jnp
from jax import lax
from jax.experimental import pallas as pl
from jax.experimental.pallas import tpu as pltpu
from jax.sharding import PartitionSpec as P

TOPK = 8
CAP = 8
RING = 4
TOK = 16
META = 128
MESH = pl.DeviceIdType.MESH
BF16 = jnp.bfloat16
F32 = jnp.float32
STEPS = (0, 1, 3, 2)
LAG = 2


def iota(shape, dim):
    return lax.broadcasted_iota(jnp.int32, shape, dim)


def routing_rows(ids, gates):
    lane = iota((TOK, META), 1)
    picked = jnp.zeros((TOK, META), F32)
    high = jnp.zeros((TOK, META), F32)
    low = jnp.zeros((TOK, META), F32)
    for k in range(TOPK):
        name = ids[:, k : k + 1]
        gate = gates[:, k : k + 1]
        picked = jnp.where(lane == name, 1.0, picked)
        high = jnp.where(lane == name + 32, gate, high)
        low = jnp.where(lane == name + 64, gate, low)
    earlier = jnp.where(iota((TOK, TOK), 1) < iota((TOK, TOK), 0), 1.0, 0.0)
    before = jnp.dot(earlier, picked, preferred_element_type=F32)
    slot = jnp.where(picked > 0.5, before, -1.0)
    low = low - low.astype(BF16).astype(F32)
    return jnp.where(lane < 32, slot, jnp.where(lane < 64, high, low)).astype(BF16)


def kernel(
    tok_hbm, ids_ref, gates_ref, wg_hbm, wu_hbm, wd_hbm, out_ref,
    wg, wu, wd, blocks, chooser, own_rows, sib_out, sib_in, meta_in, hid, mix_own, mix_sib,
    part, part_out, part_in, q, a_in, r, b_in, t, x_in,
    load_sem, blk_send, blk_recv, sel_send, sel_recv, met_send, met_recv, hid_send, hid_recv,
    prt_send, prt_recv, a_send, a_recv, b_send, b_recv, x_send, x_recv,
):
    width = wg.shape[0]
    ff = wg.shape[1]
    cols = wd.shape[1]
    group, lane_index = lax.axis_index("group"), lax.axis_index("lane")
    z, c = group // 2, lax.rem(group, 2)
    y, x = lane_index // RING, lax.rem(lane_index, RING)
    a = (1 - c) * y + c * z
    b = (1 - c) * z + c * y

    def plus(v, d):
        return lax.rem(v + d, RING)

    def device(da, dx, db):
        a2, b2 = plus(a, da), plus(b, db)
        return (((1 - c) * b2 + c * a2) * 2 + c, ((1 - c) * a2 + c * b2) * RING + plus(x, dx))

    def place(da, dx, db):
        return plus(b, db) * (RING * RING) + plus(a, da) * RING + plus(x, dx)

    sibling = (z * 2 + 1 - c, lane_index)
    own_expert = group * RING + y
    sib_expert = (z * 2 + 1 - c) * RING + y

    def remote(src, dst, send, recv, target):
        return pltpu.make_async_remote_copy(
            src_ref=src, dst_ref=dst, send_sem=send, recv_sem=recv, device_id=target, device_id_type=MESH
        )

    mine = place(0, 0, 0)
    loads = [
        pltpu.make_async_copy(tok_hbm, blocks.at[mine, :, pl.ds(0, width)], load_sem.at[0]),
        pltpu.make_async_copy(wg_hbm.at[0], wg, load_sem.at[1]),
        pltpu.make_async_copy(wu_hbm.at[0], wu, load_sem.at[2]),
        pltpu.make_async_copy(wd_hbm.at[0], wd, load_sem.at[3]),
    ]
    for load in loads:
        load.start()

    peers = [sibling]
    for d in (1, 3, 2):
        peers += [device(d, 0, 0), device(0, d, 0), device(0, 0, d)]
    barrier = pltpu.get_barrier_semaphore()
    for peer in peers:
        pl.semaphore_signal(barrier, inc=1, device_id=peer, device_id_type=MESH)

    blocks[mine, :, pl.ds(width, META)] = routing_rows(ids_ref[...], gates_ref[...])
    loads[0].wait()
    pl.semaphore_wait(barrier, len(peers))

    sent = [0]

    def send_block(s, target):
        remote(blocks.at[s], blocks.at[s], blk_send.at[sent[0]], blk_recv.at[s], target).start()
        sent[0] += 1

    def wait_block(s):
        remote(blocks.at[s], blocks.at[s], blk_send.at[0], blk_recv.at[s], sibling).wait_recv()

    order = [(dx, da) for dx in STEPS for da in STEPS]

    def forward(k):
        dx, da = order[k]
        came, goes = (3, 1) if k % 2 == 0 else (1, 3)
        s = place(da, dx, came)
        wait_block(s)
        send_block(s, device(0, 0, goes))

    for d in (1, 3, 2):
        send_block(mine, device(d, 0, 0))
    for k, (dx, da) in enumerate(order):
        s = place(da, dx, 0)
        if k > 0:
            wait_block(s)
        if dx == 0:
            for d in (1, 3, 2):
                send_block(s, device(0, d, 0))
        send_block(s, device(0, 0, 1))
        send_block(s, device(0, 0, 3))
        if k >= LAG:
            forward(k - LAG)

    def base(i):
        return plus(b, STEPS[i]) * (RING * RING)

    def select_send(i):
        return remote(sib_out, sib_in.at[i % 2], sel_send.at[i], sel_recv.at[i], sibling)

    def meta_send(i):
        return remote(
            blocks.at[pl.ds(base(i), 16), :, pl.ds(width, META)], meta_in.at[i], met_send.at[i], met_recv.at[i], sibling
        )

    def select(i):
        meta = blocks[pl.ds(base(i), 16), :, pl.ds(width, META)].reshape(256, META)
        row, lane = iota((16, META), 0), iota((16, META), 1)
        want = jnp.where(row == 0, own_expert, sib_expert)
        pick = jnp.where(lane == want, 1.0, 0.0).astype(BF16)
        slots = lax.dot_general(pick, meta, (((1,), (1,)), ((), ())), preferred_element_type=F32)
        row, col = iota((256, 256), 0), iota((256, 256), 1)
        slot = jnp.where(row < 128, slots[0:1, :], slots[1:2, :])
        same = ((row & 127) >> 3) == (col >> 4)
        taken = slot == (row & 7).astype(F32)
        chooser[...] = jnp.where(same & taken, 1.0, 0.0).astype(BF16)
        if i > 0:
            select_send(i - 1).wait_send()

        def step(j, carry):
            at = pl.ds(pl.multiple_of(j * 1024, 1024), 1024)
            rows = blocks[pl.ds(base(i), 16), :, at].reshape(256, 1024)
            got = jnp.dot(chooser[...], rows, preferred_element_type=F32).astype(BF16)
            own_rows[:, at] = got[:128]
            sib_out[:, at] = got[128:]
            return carry

        lax.fori_loop(0, width // 1024, step, 0)
        select_send(i).start()
        meta_send(i).start()

    def hid_copy(i, d):
        return remote(hid.at[i, x], hid.at[i, x], hid_send.at[i * 3 + d - 1], hid_recv.at[i * RING + x], device(0, d, 0))

    def gate_up(i):
        select_send(i).wait_recv()

        def step(n, carry):
            at = pl.ds(pl.multiple_of(n * 256, 256), 256)
            rows = jnp.concatenate([own_rows[...], sib_in[i % 2]], axis=0)
            gate = jnp.dot(rows, wg[:, at], preferred_element_type=F32)
            up = jnp.dot(rows, wu[:, at], preferred_element_type=F32)
            hid[i, x, :, at] = (gate / (1.0 + jnp.exp(-gate)) * up).astype(BF16)
            return carry

        lax.fori_loop(0, ff // 256, step, 0)
        for d in (1, 3, 2):
            hid_copy(i, d).start()

    def mixer(meta):
        lane = iota((256, META), 1)
        meta = meta.astype(F32)

        def column(at):
            return jnp.sum(jnp.where(lane == at, meta, 0.0), axis=1, keepdims=True)

        slot, high, low = column(own_expert), column(own_expert + 32), column(own_expert + 64)
        row, col = iota((256, 256), 0), iota((256, 256), 1)
        same = (row >> 4) == ((col & 127) >> 3)
        taken = slot == (col & 7).astype(F32)
        return jnp.where(same & taken, jnp.where(col < 128, high, low), 0.0).astype(BF16)

    def part_send(i):
        return remote(part_out, part_in.at[i % 2], prt_send.at[i], prt_recv.at[i], sibling)

    def finish(i):
        meta_send(i).wait_recv()
        mix_own[...] = mixer(blocks[pl.ds(base(i), 16), :, pl.ds(width, META)].reshape(256, META))
        mix_sib[...] = mixer(meta_in[i].reshape(256, META))
        for d in (1, 3, 2):
            s = plus(x, d)
            remote(hid.at[i, s], hid.at[i, s], hid_send.at[0], hid_recv.at[i * RING + s], sibling).wait_recv()
        if i > 0:
            part_send(i - 1).wait_send()

        def step(j, carry):
            at = pl.ds(pl.multiple_of(j * 256, 256), 256)
            total = jnp.zeros((256, 256), F32)
            for s in range(RING):
                total += jnp.dot(hid[i, s], wd[pl.ds(s * ff, ff), at], preferred_element_type=F32)
            total = total.astype(BF16)
            for_own = jnp.concatenate([total[:128], total[:128]], axis=0)
            for_sib = jnp.concatenate([total[128:], total[128:]], axis=0)
            part[:, at] = jnp.dot(mix_own[...], for_own, preferred_element_type=F32)
            part_out[:, at] = jnp.dot(mix_sib[...], for_sib, preferred_element_type=F32).astype(BF16)
            return carry

        lax.fori_loop(0, cols // 256, step, 0)
        part_send(i).start()

    def piece(v):
        return pl.ds(pl.multiple_of(v * 64, 64), 64)

    def a_copy(i, d):
        return remote(
            q.at[i % 2, piece(plus(a, d))], a_in.at[i, d - 1], a_send.at[i * 3 + d - 1], a_recv.at[i * 3 + d - 1], device(d, 0, 0)
        )

    def join(i):
        part_send(i).wait_recv()
        if i >= 2:
            for d in (1, 3, 2):
                a_copy(i - 2, d).wait_send()

        def step(j, carry):
            at = pl.ds(pl.multiple_of(j * 64, 64), 64)
            q[i % 2, at, :] = (part[at, :] + part_in[i % 2, at, :].astype(F32)).astype(BF16)
            return carry

        lax.fori_loop(0, RING, step, 0)
        for d in (2, 1, 3):
            a_copy(i, d).start()

    def b_copy(i):
        return remote(r.at[i], b_in.at[i - 1], b_send.at[i - 1], b_recv.at[i - 1], device(0, 0, STEPS[i]))

    def reduce_a(i):
        for d in (1, 3, 2):
            a_copy(i, d).wait_recv()
        total = q[i % 2, piece(a), :].astype(F32)
        for d in range(3):
            total += a_in[i, d].astype(F32)
        r[i] = total.astype(BF16)
        if i > 0:
            b_copy(i).start()

    def wait_chunk(i):
        for k, (dx, da) in enumerate(order):
            waited = (STEPS[i] == 3 and k % 2 == 0) or (STEPS[i] == 1 and k % 2 == 1)
            if not waited:
                wait_block(place(da, dx, STEPS[i]))

    select(0)
    for k in range(len(order) - LAG, len(order)):
        forward(k)
    loads[1].wait()
    loads[2].wait()
    gate_up(0)
    loads[3].wait()
    wait_chunk(1)
    select(1)
    finish(0)
    gate_up(1)
    join(0)
    wait_chunk(2)
    select(2)
    finish(1)
    gate_up(2)
    join(1)
    reduce_a(0)
    wait_chunk(3)
    select(3)
    finish(2)
    gate_up(3)
    join(2)
    reduce_a(1)
    finish(3)
    join(3)
    reduce_a(2)
    reduce_a(3)

    total = r[0].astype(F32)
    for i in (1, 2, 3):
        b_copy(i).wait_recv()
        total += b_in[i - 1].astype(F32)
    t[...] = total.astype(BF16)

    def x_copy(d):
        rows = pl.ds(pl.multiple_of(plus(x, d) * TOK, TOK), TOK)
        return remote(t.at[rows], x_in.at[d - 1], x_send.at[d - 1], x_recv.at[d - 1], device(0, d, 0))

    def out_cols(v):
        return pl.ds(pl.multiple_of(v * cols, 128), cols)

    for d in (2, 1, 3):
        x_copy(d).start()
    out_ref[:, out_cols(x)] = t[pl.ds(pl.multiple_of(x * TOK, TOK), TOK), :]
    for d in (1, 3, 2):
        x_copy(d).wait_recv()
        out_ref[:, out_cols(plus(x, RING - d))] = x_in[d - 1]

    for n in range(sent[0]):
        remote(blocks.at[0], blocks.at[0], blk_send.at[n], blk_recv.at[0], sibling).wait_send()
    select_send(3).wait_send()
    part_send(3).wait_send()
    for i in range(4):
        meta_send(i).wait_send()
        for d in (1, 3, 2):
            hid_copy(i, d).wait_send()
            if i >= 2:
                a_copy(i, d).wait_send()
        if i > 0:
            b_copy(i).wait_send()
            x_copy(i).wait_send()


def per_device(tokens, expert_ids, gate_weights, w_gate, w_up, w_down):
    rows, width = tokens.shape
    ff = w_gate.shape[2]
    cols = w_down.shape[2]
    dma = pltpu.SemaphoreType.DMA
    vmem = pltpu.VMEM
    return pl.pallas_call(
        kernel,
        out_shape=jax.ShapeDtypeStruct((rows, width), BF16),
        in_specs=[
            pl.BlockSpec(memory_space=pl.ANY),
            pl.BlockSpec(memory_space=pltpu.VMEM),
            pl.BlockSpec(memory_space=pltpu.VMEM),
            pl.BlockSpec(memory_space=pl.ANY),
            pl.BlockSpec(memory_space=pl.ANY),
            pl.BlockSpec(memory_space=pl.ANY),
        ],
        out_specs=pl.BlockSpec(memory_space=pltpu.VMEM),
        scratch_shapes=[
            vmem((width, ff), BF16),
            vmem((width, ff), BF16),
            vmem((RING * ff, cols), BF16),
            vmem((64, TOK, width + META), BF16),
            vmem((256, 256), BF16),
            vmem((128, width), BF16),
            vmem((128, width), BF16),
            vmem((2, 128, width), BF16),
            vmem((4, 16, TOK, META), BF16),
            vmem((4, RING, 256, ff), BF16),
            vmem((256, 256), BF16),
            vmem((256, 256), BF16),
            vmem((256, cols), F32),
            vmem((256, cols), BF16),
            vmem((2, 256, cols), BF16),
            vmem((2, 256, cols), BF16),
            vmem((4, 3, 64, cols), BF16),
            vmem((4, 64, cols), BF16),
            vmem((3, 64, cols), BF16),
            vmem((64, cols), BF16),
            vmem((3, TOK, cols), BF16),
            dma((4,)),
            dma((64,)),
            dma((64,)),
            dma((4,)),
            dma((4,)),
            dma((4,)),
            dma((4,)),
            dma((12,)),
            dma((16,)),
            dma((4,)),
            dma((4,)),
            dma((12,)),
            dma((12,)),
            dma((3,)),
            dma((3,)),
            dma((3,)),
            dma((3,)),
        ],
        compiler_params=pltpu.CompilerParams(
            collective_id=0, has_side_effects=True, vmem_limit_bytes=62 * 2**20
        ),
        cost_estimate=pl.CostEstimate(flops=24 * 10**9, bytes_accessed=24 * 10**6, transcendentals=10**6),
    )(tokens, expert_ids, gate_weights, w_gate, w_up, w_down)


def solution(mesh):
    in_specs = (
        P(("group", "lane"), None),
        P(("group", "lane"), None),
        P(("group", "lane"), None),
        P(("group", "lane"), None, None),
        P(("group", "lane"), None, None),
        P(("group", "lane"), None, None),
    )
    out_specs = P(("group", "lane"), None)
    return jax.shard_map(
        per_device, mesh=mesh, in_specs=in_specs, out_specs=out_specs, check_vma=False
    )
```

time: 361 us -> 200 us (0.55)
  Pallas kernels: 0 us -> 195 us
  blocking collectives: 176 us -> 0 us
  waiting for transfers between devices: 112 us -> 0 us
  matrix products: 41.8 us -> 0 us
  starting transfers between devices: 13.1 us -> 0 us
  local copies, waits for them, and re-layouts: 14 us -> 4.35 us
    pallas_call x0 -> x1, Pallas kernels: none -> 195 us  [per_device(): pl.pallas_call(kernel, out_shape=jax.ShapeDtypeStruct((rows, width), BF16...]
    all_to_all x1 -> x0, blocking collectives: 176 us -> none  [per_device(): lax.all_to_all(copies, ('group', 'lane'), split_axis=0, concat_axis=0, ti...]
    ppermute x2 -> x0, waiting for transfers between devices: 66.5 us -> none  [from_partner(): lax.ppermute(array, axis, [(i, i ^ 1 << distance) for i in range(lax.axis...]
    all_to_all x1 -> x0, waiting for transfers between devices: 45.7 us -> none  [per_device(): lax.all_to_all(expert_out.reshape(groups * lane_count, capacity, out_cols...]
    dot_general x5 -> x0, matrix products: 41.8 us -> none  [the longest x1 13.5 us: per_device(): jnp.dot(expert_rows, w_gate[0], preferred_element_type=jnp.float32)]
    all_to_all x1 -> x0, starting transfers between devices: 8.57 us -> none  [per_device(): lax.all_to_all(expert_out.reshape(groups * lane_count, capacity, out_cols...]
    reshape x1 -> x0, local copies, waits for them, and re-layouts: 5.74 us -> none  [per_device(): column_blocks = returned.reshape(experts, HSPLIT, capacity, out_cols)]
    ppermute x2 -> x0, starting transfers between devices: 4.51 us -> none  [from_partner(): lax.ppermute(array, axis, [(i, i ^ 1 << distance) for i in range(lax.axis...]
  transfers between devices with their start and end apart: 3 -> 0, of which waited for: 3 -> 0; matrix products, arithmetic and copies ran while one was open for 0% -> 0% of each run, Pallas kernels for 0% -> 0%
where the time goes in v1:
time: 200 us; the launch traced here: 199 us
  Pallas kernels  195 us (98%)
  local copies, waits for them, and re-layouts  4.35 us (2%)
    pallas_call x1, Pallas kernels, per_device(): pl.pallas_call(kernel, out_shape=jax.ShapeDtypeStruct((rows, width), BF16...  195 us
    unnamed x3, local copies, waits for them, and re-layouts  4.35 us

profile of v1, /device:TPU:1, one launch (start us, length us, event | category | flops | bytes accessed | tf_op | source)
XLA Modules:
  0.0 199.4 jit_solution(16674688572351482995)
XLA Ops:
  0.0 1.4 copy.7.ids_ref
  1.4 1.4 copy.8.gates_ref
  2.7 195.1 %shard_map.64 = bf16[16,7168]{1,0:T(8,128)(2,1)} custom-call(bf16[16,7168]{1,0:T(8,128)(2,1)} %tok_hbm.1, s32[16,8]{1,0:T(8,128)} %copy.7.ids_ref, f32[16,8]{1,0:T(8,128)} %copy.8.gates_ref, bf16[1,7168,512]{2,1,0:T(8,128)(2,1)} %wg_hbm.1, bf16[1,7168,512]{2,1,0:T(8,128)(2,1)} %wu_hbm.1, bf16[1,2048,1792]{2,1,0:T(8,128)(2,1)} %wd_hbm.1), custom_call_target="tpu_custom_call" | custom-call | flops 24000000000 | bytes 24000000 | tf_op jit(solution)/shard_map/pallas_call | solution.py:338
  197.8 1.6 copy.10

commit v2 on v1

v2 whole, which is shorter than its diff:
```python
import jax
import jax.numpy as jnp
from jax import lax
from jax.experimental import pallas as pl
from jax.experimental.pallas import tpu as pltpu
from jax.sharding import PartitionSpec as P

TOPK = 8
CAP = 8
RING = 4
TOK = 16
META = 128
MESH = pl.DeviceIdType.MESH
BF16 = jnp.bfloat16
F32 = jnp.float32
STEPS = (0, 1, 3, 2)


def iota(shape, dim):
    return lax.broadcasted_iota(jnp.int32, shape, dim)


def routing_rows(ids, gates):
    unit = jnp.where(iota((TOPK, TOPK), 0) == iota((TOPK, TOPK), 1), 1.0, 0.0).astype(BF16)

    def turned(values):
        return lax.dot_general(values.astype(BF16), unit, (((0,), (0,)), ((), ())), preferred_element_type=F32)

    ids = turned(ids.astype(F32)).astype(jnp.int32)
    upper = gates.astype(BF16).astype(F32)
    lower = turned(gates - upper)
    upper = turned(upper)
    lane = iota((TOK, META), 1)
    picked = jnp.zeros((TOK, META), F32)
    high = jnp.zeros((TOK, META), F32)
    low = jnp.zeros((TOK, META), F32)
    for k in range(TOPK):
        name = ids[:, k : k + 1]
        picked = jnp.where(lane == name, 1.0, picked)
        high = jnp.where(lane == name + 32, upper[:, k : k + 1], high)
        low = jnp.where(lane == name + 64, lower[:, k : k + 1], low)
    earlier = jnp.where(iota((TOK, TOK), 1) < iota((TOK, TOK), 0), 1.0, 0.0)
    before = jnp.dot(earlier, picked, preferred_element_type=F32)
    slot = jnp.where(picked > 0.5, before, -1.0)
    return jnp.where(lane < 32, slot, jnp.where(lane < 64, high, low)).astype(BF16)


def kernel(
    tok_hbm, ids_ref, gates_ref, wg_hbm, wu_hbm, wd_hbm, out_ref,
    wg, wu, wd, blocks, chooser, rows, sib_out, meta_in, hid, mix_own, mix_sib,
    part, part_out, part_in, q, b_in, r, a_in, last, x_in,
    load_sem, blk_send, blk_recv, sel_send, sel_recv, met_send, met_recv, hid_send, hid_recv,
    prt_send, prt_recv, b_send, b_recv, a_send, a_recv, x_send, x_recv,
):
    width = wg.shape[0]
    ff = wg.shape[1]
    cols = wd.shape[1]
    group, lane_index = lax.axis_index("group"), lax.axis_index("lane")
    z, c = group // 2, lax.rem(group, 2)
    y, x = lane_index // RING, lax.rem(lane_index, RING)
    a = (1 - c) * y + c * z
    b = (1 - c) * z + c * y

    def plus(v, d):
        return lax.rem(v + d, RING)

    def device(da, dx, db):
        a2, b2 = plus(a, da), plus(b, db)
        return (((1 - c) * b2 + c * a2) * 2 + c, ((1 - c) * a2 + c * b2) * RING + plus(x, dx))

    def place(da, dx, db):
        return plus(a, da) * (RING * RING) + plus(b, db) * RING + plus(x, dx)

    sibling = (z * 2 + 1 - c, lane_index)
    own_expert = group * RING + y
    sib_expert = (z * 2 + 1 - c) * RING + y

    def remote(src, dst, send, recv, target):
        return pltpu.make_async_remote_copy(
            src_ref=src, dst_ref=dst, send_sem=send, recv_sem=recv, device_id=target, device_id_type=MESH
        )

    mine = place(0, 0, 0)
    loads = [
        pltpu.make_async_copy(tok_hbm, blocks.at[mine, :, pl.ds(0, width)], load_sem.at[0]),
        pltpu.make_async_copy(wg_hbm.at[0], wg, load_sem.at[1]),
        pltpu.make_async_copy(wu_hbm.at[0], wu, load_sem.at[2]),
        pltpu.make_async_copy(wd_hbm.at[0], wd, load_sem.at[3]),
    ]
    for load in loads:
        load.start()

    peers = [sibling]
    for d in (1, 3, 2):
        peers += [device(d, 0, 0), device(0, d, 0), device(0, 0, d)]
    barrier = pltpu.get_barrier_semaphore()
    for peer in peers:
        pl.semaphore_signal(barrier, inc=1, device_id=peer, device_id_type=MESH)

    blocks[mine, :, pl.ds(width, META)] = routing_rows(ids_ref[...], gates_ref[...])
    loads[0].wait()
    pl.semaphore_wait(barrier, len(peers))

    sent = [0]
    order = [(da, dx) for da in STEPS for dx in STEPS]

    def send_block(s, target):
        remote(blocks.at[s], blocks.at[s], blk_send.at[sent[0]], blk_recv.at[s], target).start()
        sent[0] += 1

    def wait_block(s):
        remote(blocks.at[s], blocks.at[s], blk_send.at[0], blk_recv.at[s], sibling).wait_recv()

    def along_x(i):
        s = place(STEPS[i], 0, 0)
        if i > 0:
            wait_block(s)
        send_block(s, device(0, 1, 0))
        send_block(s, device(0, 3, 0))

    def own(k):
        da, dx = order[k]
        s = place(da, dx, 0)
        if dx != 0:
            wait_block(s)
        if dx == (3, 1)[k // RING % 2]:
            send_block(s, device(0, RING - dx, 0))
        send_block(s, device(0, 0, 1))
        send_block(s, device(0, 0, 3))

    def forward(k):
        da, dx = order[k]
        came, goes = (3, 1) if k % 2 == 0 else (1, 3)
        s = place(da, dx, came)
        wait_block(s)
        send_block(s, device(0, 0, goes))

    def wait_chunk(i):
        for k in range(i * RING, i * RING + RING):
            da, dx = order[k]
            for db in (1, 3, 2):
                if db != (3, 1)[k % 2]:
                    wait_block(place(da, dx, db))

    def base(i):
        return plus(a, STEPS[i]) * (RING * RING)

    def select_send(i):
        return remote(sib_out, rows.at[i % 2, pl.ds(128, 128)], sel_send.at[i], sel_recv.at[i], sibling)

    def meta_send(i):
        return remote(
            blocks.at[pl.ds(base(i), 16), :, pl.ds(width, META)], meta_in.at[i], met_send.at[i], met_recv.at[i], sibling
        )

    def select(i):
        meta = blocks[pl.ds(base(i), 16), :, pl.ds(width, META)].reshape(256, META)
        row, lane = iota((16, META), 0), iota((16, META), 1)
        want = jnp.where(row == 0, own_expert, sib_expert)
        pick = jnp.where(lane == want, 1.0, 0.0).astype(BF16)
        slots = lax.dot_general(pick, meta, (((1,), (1,)), ((), ())), preferred_element_type=F32)
        row, col = iota((256, 256), 0), iota((256, 256), 1)
        slot = jnp.where(row < 128, slots[0:1, :], slots[1:2, :])
        same = ((row & 127) >> 3) == (col >> 4)
        taken = slot == (row & 7).astype(F32)
        chooser[...] = jnp.where(same & taken, 1.0, 0.0).astype(BF16)
        if i > 0:
            select_send(i - 1).wait_send()

        def step(j, carry):
            at = pl.ds(pl.multiple_of(j * 1024, 1024), 1024)
            tokens = blocks[pl.ds(base(i), 16), :, at].reshape(256, 1024)
            got = jnp.dot(chooser[...], tokens, preferred_element_type=F32).astype(BF16)
            rows[i % 2, pl.ds(0, 128), at] = got[:128]
            sib_out[:, at] = got[128:]
            return carry

        lax.fori_loop(0, width // 1024, step, 0)
        select_send(i).start()
        meta_send(i).start()

    def hid_copy(i, owner, h, target, n):
        at = hid.at[i, owner, pl.ds(h * 128, 128)]
        return remote(at, at, hid_send.at[i * 6 + n], hid_recv.at[(i * RING + owner) * 2 + h], device(0, target, 0))

    def gate_up(i):
        select_send(i).wait_recv()

        def step(n, carry):
            at = pl.ds(pl.multiple_of(n * 256, 256), 256)
            gate = jnp.dot(rows[i % 2], wg[:, at], preferred_element_type=F32)
            up = jnp.dot(rows[i % 2], wu[:, at], preferred_element_type=F32)
            hid[i, x, :, at] = (gate / (1.0 + jnp.exp(-gate)) * up).astype(BF16)
            return carry

        lax.fori_loop(0, ff // 256, step, 0)
        hid_copy(i, x, 0, 1, 0).start()
        hid_copy(i, x, 1, 3, 1).start()
        hid_copy(i, x, 1, 1, 2).start()
        hid_copy(i, x, 0, 3, 3).start()

    def hid_forward(i):
        hid_copy(i, plus(x, 3), 0, 1, 4).wait_recv()
        hid_copy(i, plus(x, 3), 0, 1, 4).start()
        hid_copy(i, plus(x, 1), 1, 3, 5).wait_recv()
        hid_copy(i, plus(x, 1), 1, 3, 5).start()

    def mixer(meta):
        lane = iota((256, META), 1)
        meta = meta.astype(F32)

        def column(at):
            return jnp.sum(jnp.where(lane == at, meta, 0.0), axis=1, keepdims=True)

        slot, high, low = column(own_expert), column(own_expert + 32), column(own_expert + 64)
        row, col = iota((256, 256), 0), iota((256, 256), 1)
        same = (row >> 4) == ((col & 127) >> 3)
        taken = slot == (col & 7).astype(F32)
        return jnp.where(same & taken, jnp.where(col < 128, high, low), 0.0).astype(BF16)

    def part_send(i):
        return remote(part_out, part_in.at[i % 2], prt_send.at[i], prt_recv.at[i], sibling)

    def finish(i):
        meta_send(i).wait_recv()
        mix_own[...] = mixer(blocks[pl.ds(base(i), 16), :, pl.ds(width, META)].reshape(256, META))
        mix_sib[...] = mixer(meta_in[i].reshape(256, META))
        hid_copy(i, plus(x, 3), 1, 1, 0).wait_recv()
        hid_copy(i, plus(x, 1), 0, 1, 0).wait_recv()
        hid_copy(i, plus(x, 2), 0, 1, 0).wait_recv()
        hid_copy(i, plus(x, 2), 1, 1, 0).wait_recv()
        if i > 0:
            part_send(i - 1).wait_send()

        def step(j, carry):
            at = pl.ds(pl.multiple_of(j * 896, 896), 896)
            hidden = jnp.concatenate([hid[i, s] for s in range(RING)], axis=1)
            total = jnp.dot(hidden, wd[:, at], preferred_element_type=F32).astype(BF16)
            for_own = jnp.concatenate([total[:128], total[:128]], axis=0)
            for_sib = jnp.concatenate([total[128:], total[128:]], axis=0)
            part_out[:, at] = jnp.dot(mix_sib[...], for_sib, preferred_element_type=F32).astype(BF16)
            part[:, at] = jnp.dot(mix_own[...], for_own, preferred_element_type=F32).astype(BF16)
            return carry

        lax.fori_loop(0, cols // 896, step, 0)
        part_send(i).start()

    def b_copy(i, d):
        at = pl.ds(pl.multiple_of(plus(b, d) * 64, 64), 64)
        n = i * 3 + d - 1
        return remote(q.at[i % 2, at], b_in.at[i, d - 1], b_send.at[n], b_recv.at[n], device(0, 0, d))

    def join(i):
        part_send(i).wait_recv()
        if i >= 2:
            for d in (1, 3, 2):
                b_copy(i - 2, d).wait_send()

        def step(j, carry):
            at = pl.ds(pl.multiple_of(j * 64, 64), 64)
            q[i % 2, at, :] = (part[at, :].astype(F32) + part_in[i % 2, at, :].astype(F32)).astype(BF16)
            return carry

        lax.fori_loop(0, RING, step, 0)
        for d in (2, 1, 3):
            b_copy(i, d).start()

    def a_copy(i):
        return remote(r.at[i], a_in.at[i - 1], a_send.at[i - 1], a_recv.at[i - 1], device(STEPS[i], 0, 0))

    def reduce_b(i):
        for d in (1, 3, 2):
            b_copy(i, d).wait_recv()
        total = q[i % 2, pl.ds(pl.multiple_of(b * 64, 64), 64), :].astype(F32)
        for d in range(3):
            total += b_in[i, d].astype(F32)
        r[i] = total.astype(BF16)
        if i > 0:
            a_copy(i).start()

    def x_copy(d):
        at = pl.ds(pl.multiple_of(plus(x, d) * TOK, TOK), TOK)
        return remote(last.at[at], x_in.at[d - 1], x_send.at[d - 1], x_recv.at[d - 1], device(0, d, 0))

    def out_cols(v):
        return pl.ds(pl.multiple_of(v * cols, 128), cols)

    own(0)
    along_x(0)
    for d in (1, 3, 2):
        send_block(mine, device(d, 0, 0))
    own(1)
    forward(0)
    own(2)
    along_x(1)
    forward(1)
    own(4)
    own(3)
    forward(2)
    along_x(2)
    own(5)
    forward(3)
    own(6)
    forward(4)
    wait_chunk(0)
    select(0)
    along_x(3)
    own(7)
    forward(5)
    own(8)
    forward(6)
    loads[1].wait()
    loads[2].wait()
    gate_up(0)
    own(9)
    forward(7)
    own(10)
    forward(8)
    wait_chunk(1)
    select(1)
    hid_forward(0)
    own(11)
    forward(9)
    own(12)
    forward(10)
    gate_up(1)
    own(13)
    forward(11)
    loads[3].wait()
    finish(0)
    own(14)
    forward(12)
    wait_chunk(2)
    select(2)
    hid_forward(1)
    own(15)
    forward(13)
    join(0)
    gate_up(2)
    forward(14)
    forward(15)
    finish(1)
    reduce_b(0)
    wait_chunk(3)
    select(3)
    join(1)
    hid_forward(2)
    gate_up(3)
    finish(2)
    join(2)
    reduce_b(1)
    hid_forward(3)
    reduce_b(2)
    finish(3)
    join(3)
    reduce_b(3)

    total = r[0].astype(F32)
    for i in (1, 2, 3):
        a_copy(i).wait_recv()
        total += a_in[i - 1].astype(F32)
    last[...] = total.astype(BF16)
    for d in (2, 1, 3):
        x_copy(d).start()
    out_ref[:, out_cols(x)] = last[pl.ds(pl.multiple_of(x * TOK, TOK), TOK), :]
    for d in (1, 3, 2):
        x_copy(d).wait_recv()
        out_ref[:, out_cols(plus(x, RING - d))] = x_in[d - 1]

    for n in range(sent[0]):
        remote(blocks.at[0], blocks.at[0], blk_send.at[n], blk_recv.at[0], sibling).wait_send()
    select_send(3).wait_send()
    part_send(3).wait_send()
    for i in range(4):
        meta_send(i).wait_send()
        for n in range(6):
            hid_copy(i, x, 0, 1, n).wait_send()
        if i >= 2:
            for d in (1, 3, 2):
                b_copy(i, d).wait_send()
        if i > 0:
            a_copy(i).wait_send()
            x_copy(i).wait_send()


def per_device(tokens, expert_ids, gate_weights, w_gate, w_up, w_down):
    rows, width = tokens.shape
    ff = w_gate.shape[2]
    cols = w_down.shape[2]
    dma = pltpu.SemaphoreType.DMA
    vmem = pltpu.VMEM
    return pl.pallas_call(
        kernel,
        out_shape=jax.ShapeDtypeStruct((rows, width), BF16),
        in_specs=[
            pl.BlockSpec(memory_space=pl.ANY),
            pl.BlockSpec(memory_space=pltpu.VMEM),
            pl.BlockSpec(memory_space=pltpu.VMEM),
            pl.BlockSpec(memory_space=pl.ANY),
            pl.BlockSpec(memory_space=pl.ANY),
            pl.BlockSpec(memory_space=pl.ANY),
        ],
        out_specs=pl.BlockSpec(memory_space=pltpu.VMEM),
        scratch_shapes=[
            vmem((width, ff), BF16),
            vmem((width, ff), BF16),
            vmem((RING * ff, cols), BF16),
            vmem((64, TOK, width + META), BF16),
            vmem((256, 256), BF16),
            vmem((2, 256, width), BF16),
            vmem((128, width), BF16),
            vmem((4, 16, TOK, META), BF16),
            vmem((4, RING, 256, ff), BF16),
            vmem((256, 256), BF16),
            vmem((256, 256), BF16),
            vmem((256, cols), BF16),
            vmem((256, cols), BF16),
            vmem((2, 256, cols), BF16),
            vmem((2, 256, cols), BF16),
            vmem((4, 3, 64, cols), BF16),
            vmem((4, 64, cols), BF16),
            vmem((3, 64, cols), BF16),
            vmem((64, cols), BF16),
            vmem((3, TOK, cols), BF16),
            dma((4,)),
            dma((64,)),
            dma((64,)),
            dma((4,)),
            dma((4,)),
            dma((4,)),
            dma((4,)),
            dma((24,)),
            dma((32,)),
            dma((4,)),
            dma((4,)),
            dma((12,)),
            dma((12,)),
            dma((3,)),
            dma((3,)),
            dma((3,)),
            dma((3,)),
        ],
        compiler_params=pltpu.CompilerParams(
            collective_id=0, has_side_effects=True, vmem_limit_bytes=63 * 2**20
        ),
        cost_estimate=pl.CostEstimate(flops=24 * 10**9, bytes_accessed=24 * 10**6, transcendentals=10**6),
    )(tokens, expert_ids.T, gate_weights.T, w_gate, w_up, w_down)


def solution(mesh):
    in_specs = (
        P(("group", "lane"), None),
        P(("group", "lane"), None),
        P(("group", "lane"), None),
        P(("group", "lane"), None, None),
        P(("group", "lane"), None, None),
        P(("group", "lane"), None, None),
    )
    out_specs = P(("group", "lane"), None)
    return jax.shard_map(
        per_device, mesh=mesh, in_specs=in_specs, out_specs=out_specs, check_vma=False
    )
```

time: 200 us -> 144 us (0.72)
  Pallas kernels: 195 us -> 142 us
  local copies, waits for them, and re-layouts: 4.35 us -> 1.64 us
    pallas_call x1, Pallas kernels: 195 us -> 142 us  [per_device(): pl.pallas_call(kernel, out_shape=jax.ShapeDtypeStruct((rows, width), BF16...]
    unnamed x3 -> x1, local copies, waits for them, and re-layouts: 4.35 us -> 1.64 us
where the time goes in v2:
time: 144 us; the launch traced here: 143 us
  Pallas kernels  142 us (99%)
  local copies, waits for them, and re-layouts  1.64 us (1%)
    pallas_call x1, Pallas kernels, per_device(): pl.pallas_call(kernel, out_shape=jax.ShapeDtypeStruct((rows, width), BF16...  142 us

profile of v2, /device:TPU:1, one launch (start us, length us, event | category | flops | bytes accessed | tf_op | source)
XLA Modules:
  0.0 143.3 jit_solution(3199854337559639654)
XLA Ops:
  0.0 141.7 %shard_map.64 = bf16[16,7168]{1,0:T(8,128)(2,1)} custom-call(bf16[16,7168]{1,0:T(8,128)(2,1)} %tok_hbm.1, s32[8,16]{1,0:T(8,128)} %bitcast.2, f32[8,16]{1,0:T(8,128)} %bitcast.3, bf16[1,7168,512]{2,1,0:T(8,128)(2,1)} %wg_hbm.1, bf16[1,7168,512]{2,1,0:T(8,128)(2,1)} %wu_hbm.1, bf16[1,2048,1792]{2,1,0:T(8,128)(2,1)} %wd_hbm.1), custom_call_target="tpu_custom_call" | custom-call | flops 24000000000 | bytes 24000000 | tf_op jit(solution)/shard_map/pallas_call | solution.py:392
  141.7 1.6 %copy.8 = bf16[16,7168]{1,0:T(8,128)(2,1)} copy(bf16[16,7168]{1,0:T(8,128)(2,1)} %shard_map.64) | data formatting | bytes 458752

commit v3 on v2

v3 whole, which is shorter than its diff:
```python
import jax
import jax.numpy as jnp
from jax import lax
from jax.experimental import pallas as pl
from jax.experimental.pallas import tpu as pltpu
from jax.sharding import PartitionSpec as P

TOPK = 8
CAP = 8
RING = 4
TOK = 16
META = 128
MESH = pl.DeviceIdType.MESH
BF16 = jnp.bfloat16
F32 = jnp.float32
STEPS = (0, 1, 3, 2)
CHUNKS = (1, 3, 2, 0)


def iota(shape, dim):
    return lax.broadcasted_iota(jnp.int32, shape, dim)


def routing_rows(ids, gates):
    unit = jnp.where(iota((TOPK, TOPK), 0) == iota((TOPK, TOPK), 1), 1.0, 0.0).astype(BF16)

    def turned(values):
        return lax.dot_general(values.astype(BF16), unit, (((0,), (0,)), ((), ())), preferred_element_type=F32)

    ids = turned(ids.astype(F32)).astype(jnp.int32)
    upper = gates.astype(BF16).astype(F32)
    lower = turned(gates - upper)
    upper = turned(upper)
    lane = iota((TOK, META), 1)
    picked = jnp.zeros((TOK, META), F32)
    high = jnp.zeros((TOK, META), F32)
    low = jnp.zeros((TOK, META), F32)
    for k in range(TOPK):
        name = ids[:, k : k + 1]
        picked = jnp.where(lane == name, 1.0, picked)
        high = jnp.where(lane == name + 32, upper[:, k : k + 1], high)
        low = jnp.where(lane == name + 64, lower[:, k : k + 1], low)
    earlier = jnp.where(iota((TOK, TOK), 1) < iota((TOK, TOK), 0), 1.0, 0.0)
    before = jnp.dot(earlier, picked, preferred_element_type=F32)
    slot = jnp.where(picked > 0.5, before, -1.0)
    return jnp.where(lane < 32, slot, jnp.where(lane < 64, high, low)).astype(BF16)


def kernel(
    tok_hbm, ids_ref, gates_ref, wg_hbm, wu_hbm, wd_hbm, out_ref,
    wg, wu, wd, blocks, chooser, rows, sib_out, meta_in, hid, mix_own, mix_sib,
    part, part_out, part_in, q, b_in, r, a_in, last, x_in,
    load_sem, blk_send, blk_recv, sel_send, sel_recv, met_send, met_recv, hid_send, hid_recv,
    prt_send, prt_recv, b_send, b_recv, a_send, a_recv, x_send, x_recv,
):
    width = wg.shape[0]
    ff = wg.shape[1]
    cols = wd.shape[1]
    half = cols // 2
    group, lane_index = lax.axis_index("group"), lax.axis_index("lane")
    z, c = group // 2, lax.rem(group, 2)
    y, x = lane_index // RING, lax.rem(lane_index, RING)
    a = (1 - c) * y + c * z
    b = (1 - c) * z + c * y

    def plus(v, d):
        return lax.rem(v + d, RING)

    def device(da, dx, db):
        a2, b2 = plus(a, da), plus(b, db)
        return (((1 - c) * b2 + c * a2) * 2 + c, ((1 - c) * a2 + c * b2) * RING + plus(x, dx))

    def place(da, dx, db):
        return plus(a, da) * (RING * RING) + plus(x, dx) * RING + plus(b, db)

    sibling = (z * 2 + 1 - c, lane_index)
    own_expert = group * RING + y
    sib_expert = (z * 2 + 1 - c) * RING + y

    def remote(src, dst, send, recv, target):
        return pltpu.make_async_remote_copy(
            src_ref=src, dst_ref=dst, send_sem=send, recv_sem=recv, device_id=target, device_id_type=MESH
        )

    mine = place(0, 0, 0)
    loads = [
        pltpu.make_async_copy(tok_hbm, blocks.at[mine, :, pl.ds(0, width)], load_sem.at[0]),
        pltpu.make_async_copy(wg_hbm.at[0], wg, load_sem.at[1]),
        pltpu.make_async_copy(wu_hbm.at[0], wu, load_sem.at[2]),
        pltpu.make_async_copy(wd_hbm.at[0], wd, load_sem.at[3]),
    ]
    for load in loads:
        load.start()

    peers = [sibling]
    for d in (1, 3, 2):
        peers += [device(d, 0, 0), device(0, d, 0), device(0, 0, d)]
    barrier = pltpu.get_barrier_semaphore()
    for peer in peers:
        pl.semaphore_signal(barrier, inc=1, device_id=peer, device_id_type=MESH)

    blocks[mine, :, pl.ds(width, META)] = routing_rows(ids_ref[...], gates_ref[...])
    loads[0].wait()
    pl.semaphore_wait(barrier, len(peers))

    sent = [0]
    order = [(da, dx) for da in CHUNKS for dx in STEPS]

    def send_block(s, target):
        remote(blocks.at[s], blocks.at[s], blk_send.at[sent[0]], blk_recv.at[s], target).start()
        sent[0] += 1

    def wait_block(s):
        remote(blocks.at[s], blocks.at[s], blk_send.at[0], blk_recv.at[s], sibling).wait_recv()

    def along_x(i):
        s = place(CHUNKS[i], 0, 0)
        if CHUNKS[i] != 0:
            wait_block(s)
        send_block(s, device(0, 1, 0))
        send_block(s, device(0, 3, 0))

    def spot(k, db):
        da, dx = order[k]
        if k < 3 * RING:
            return place(da, dx, db)
        return plus(a, da) * (RING * RING) + (k % RING) * RING + plus(b, db)

    def across(k):
        da, dx = order[k]
        s = place(da, dx, 0)
        if dx != 0:
            wait_block(s)
        if dx == (3, 1)[k // RING % 2]:
            send_block(s, device(0, RING - dx, 0))

    def own(k):
        if k < 3 * RING:
            across(k)
        s = spot(k, 0)
        send_block(s, device(0, 0, 1))
        send_block(s, device(0, 0, 3))

    def forward(k):
        came, goes = (3, 1) if k % 2 == 0 else (1, 3)
        s = spot(k, came)
        wait_block(s)
        send_block(s, device(0, 0, goes))

    blocks_in = (16, 16, 16, 8, 8)
    chunk_of = (0, 1, 2, 3, 3)
    first = (0, 0, 0, 0, 2)

    def wait_chunk(i):
        begin = chunk_of[i] * RING + first[i]
        for k in range(begin, begin + blocks_in[i] // RING):
            for db in (1, 3, 2):
                if db != (3, 1)[k % 2]:
                    wait_block(spot(k, db))

    def chunk(i):
        return pl.ds(plus(a, CHUNKS[chunk_of[i]]) * (RING * RING) + first[i] * RING, blocks_in[i])

    def over_x(i):
        return pl.ds(first[i], blocks_in[i] // RING)

    def select_send(i):
        n = blocks_in[i] * CAP
        return remote(sib_out.at[pl.ds(0, n)], rows.at[i % 2, pl.ds(n, n)], sel_send.at[i], sel_recv.at[i], sibling)

    def meta_send(i):
        return remote(
            blocks.at[chunk(i), :, pl.ds(width, META)], meta_in.at[i, pl.ds(0, blocks_in[i])], met_send.at[i], met_recv.at[i], sibling
        )

    def select(i):
        n, m = blocks_in[i] * CAP, blocks_in[i] * TOK
        meta = blocks[chunk(i), :, pl.ds(width, META)].reshape(m, META)
        row, lane = iota((16, META), 0), iota((16, META), 1)
        want = jnp.where(row == 0, own_expert, sib_expert)
        pick = jnp.where(lane == want, 1.0, 0.0).astype(BF16)
        slots = lax.dot_general(pick, meta, (((1,), (1,)), ((), ())), preferred_element_type=F32)
        row, col = iota((m, m), 0), iota((m, m), 1)
        slot = jnp.where(row < n, slots[0:1, :], slots[1:2, :])
        same = ((row & (n - 1)) >> 3) == (col >> 4)
        taken = slot == (row & 7).astype(F32)
        chooser[pl.ds(0, m), pl.ds(0, m)] = jnp.where(same & taken, 1.0, 0.0).astype(BF16)
        if i > 0:
            select_send(i - 1).wait_send()

        def step(j, carry):
            at = pl.ds(pl.multiple_of(j * 1024, 1024), 1024)
            tokens = blocks[chunk(i), :, at].reshape(m, 1024)
            got = jnp.dot(chooser[pl.ds(0, m), pl.ds(0, m)], tokens, preferred_element_type=F32).astype(BF16)
            rows[i % 2, pl.ds(0, n), at] = got[:n]
            sib_out[pl.ds(0, n), at] = got[n:]
            return carry

        lax.fori_loop(0, width // 1024, step, 0)
        select_send(i).start()
        meta_send(i).start()

    def hid_rows(i):
        return pl.ds(first[i] * 64, blocks_in[i] * TOK)

    def hid_copy(i, owner, h, target, n):
        at = hid.at[chunk_of[i], owner, h, hid_rows(i)]
        return remote(at, at, hid_send.at[i * 6 + n], hid_recv.at[(i * RING + owner) * 2 + h], device(0, target, 0))

    def gate_up(i, h):
        if h == 0:
            select_send(i).wait_recv()
        at = pl.ds(h * 256, 256)
        chosen = rows.at[i % 2, pl.ds(0, blocks_in[i] * TOK)]
        gate = jnp.dot(chosen[...], wg[:, at], preferred_element_type=F32)
        up = jnp.dot(chosen[...], wu[:, at], preferred_element_type=F32)
        hid[chunk_of[i], x, h, hid_rows(i)] = (gate / (1.0 + jnp.exp(-gate)) * up).astype(BF16)
        hid_copy(i, x, h, (1, 3)[h], h).start()
        hid_copy(i, x, h, (3, 1)[h], 2 + h).start()

    def hid_forward(i, h):
        came, goes = ((3, 1), (1, 3))[h]
        hid_copy(i, plus(x, came), h, goes, 4 + h).wait_recv()
        hid_copy(i, plus(x, came), h, goes, 4 + h).start()

    def mixer(meta, n, m):
        meta = meta.reshape(m, META).astype(F32)
        lane = iota((m, META), 1)

        def column(at):
            return jnp.sum(jnp.where(lane == at, meta, 0.0), axis=1, keepdims=True)

        slot, high, low = column(own_expert), column(own_expert + 32), column(own_expert + 64)
        row, col = iota((m, m), 0), iota((m, m), 1)
        same = (row >> 4) == ((col & (n - 1)) >> 3)
        taken = slot == (col & 7).astype(F32)
        return jnp.where(same & taken, jnp.where(col < n, high, low), 0.0).astype(BF16)

    def part_send(i, j):
        n, count = i * 2 + j, pl.ds(0, blocks_in[i] // RING)
        return remote(part_out.at[j, count], part_in.at[i % 2, j, count], prt_send.at[n], prt_recv.at[n], sibling)

    def weigh(i):
        n, m = blocks_in[i] * CAP, blocks_in[i] * TOK
        meta_send(i).wait_recv()
        at = pl.ds(0, m)
        mix_own[at, at] = mixer(blocks[chunk(i), :, pl.ds(width, META)], n, m)
        mix_sib[at, at] = mixer(meta_in[i, pl.ds(0, blocks_in[i])], n, m)

    def finish(i, j):
        if j == 0:
            hid_copy(i, plus(x, 3), 1, 1, 0).wait_recv()
            hid_copy(i, plus(x, 1), 0, 1, 0).wait_recv()
            hid_copy(i, plus(x, 2), 0, 1, 0).wait_recv()
            hid_copy(i, plus(x, 2), 1, 1, 0).wait_recv()
        n, m = blocks_in[i] * CAP, blocks_in[i] * TOK
        at, count = pl.ds(0, m), pl.ds(0, blocks_in[i] // RING)
        shape = (blocks_in[i] // RING, RING, TOK, half)
        hidden = jnp.concatenate([hid[chunk_of[i], s, h, hid_rows(i)] for s in range(RING) for h in range(2)], axis=1)
        total = jnp.dot(hidden, wd[:, pl.ds(j * half, half)], preferred_element_type=F32).astype(BF16)
        for_own = jnp.concatenate([total[:n], total[:n]], axis=0)
        for_sib = jnp.concatenate([total[n:], total[n:]], axis=0)
        if i > 0:
            part_send(i - 1, j).wait_send()
        mixed = jnp.dot(mix_sib[at, at], for_sib, preferred_element_type=F32).astype(BF16)
        part_out[j, count] = mixed.reshape(shape)
        part_send(i, j).start()
        mixed = jnp.dot(mix_own[at, at], for_own, preferred_element_type=F32).astype(BF16)
        part[j, count] = mixed.reshape(shape)

    def b_copy(i, d, j):
        n = (i * 3 + d - 1) * 2 + j
        return remote(
            q.at[i % 2, j, pl.ds(0, blocks_in[i] // RING), plus(b, d)], b_in.at[chunk_of[i], d - 1, j, over_x(i)],
            b_send.at[n], b_recv.at[n], device(0, 0, d),
        )

    def join(i, j):
        part_send(i, j).wait_recv()
        if i >= 2:
            for d in (1, 3, 2):
                b_copy(i - 2, d, j).wait_send()

        def step(n, carry):
            q[i % 2, j, n] = (part[j, n].astype(F32) + part_in[i % 2, j, n].astype(F32)).astype(BF16)
            return carry

        lax.fori_loop(0, blocks_in[i] // RING, step, 0)
        for d in (2, 1, 3):
            b_copy(i, d, j).start()

    def a_copy(i, j):
        n = i * 2 + j
        return remote(r.at[i, j], a_in.at[i, j], a_send.at[n], a_recv.at[n], device(CHUNKS[i], 0, 0))

    def reduce(i, j):
        for d in (1, 3, 2):
            b_copy(i, d, j).wait_recv()
        total = q[i % 2, j, pl.ds(0, blocks_in[i] // RING), b].astype(F32)
        for d in range(3):
            total += b_in[chunk_of[i], d, j, over_x(i)].astype(F32)
        if i < 3:
            r[i, j] = total.astype(BF16)
            a_copy(i, j).start()
            return
        for n in range(3):
            if i == 3:
                a_copy(n, j).wait_recv()
            total += a_in[n, j, over_x(i)].astype(F32)
        last[j, over_x(i)] = total.astype(BF16)
        if i == 4:
            for d in (2, 1, 3):
                x_copy(d, j).start()

    def x_copy(d, j):
        n = (d - 1) * 2 + j
        return remote(last.at[j, plus(x, d)], x_in.at[d - 1, j], x_send.at[n], x_recv.at[n], device(0, d, 0))

    def out_cols(v, j):
        return pl.ds(pl.multiple_of(v * cols + j * half, 128), half)

    for d in (3, 1, 2):
        send_block(mine, device(d, 0, 0))
    along_x(0)
    own(0)
    own(1)
    forward(0)
    own(2)
    along_x(1)
    forward(1)
    own(4)
    own(3)
    forward(2)
    along_x(2)
    own(5)
    forward(3)
    own(6)
    forward(4)
    along_x(3)
    own(7)
    forward(5)
    own(8)
    forward(6)
    wait_chunk(0)
    select(0)
    own(9)
    forward(7)
    own(10)
    forward(8)
    loads[1].wait()
    loads[2].wait()
    gate_up(0, 0)
    across(13)
    across(14)
    own(11)
    forward(9)
    gate_up(0, 1)
    across(15)
    own(12)
    forward(10)
    wait_chunk(1)
    select(1)
    hid_forward(0, 0)
    own(13)
    forward(11)
    hid_forward(0, 1)
    own(14)
    forward(12)
    gate_up(1, 0)
    own(15)
    forward(13)
    gate_up(1, 1)
    forward(14)
    wait_chunk(2)
    select(2)
    forward(15)
    hid_forward(1, 0)
    weigh(0)
    loads[3].wait()
    finish(0, 0)
    finish(0, 1)
    hid_forward(1, 1)
    gate_up(2, 0)
    gate_up(2, 1)
    wait_chunk(3)
    select(3)
    join(0, 0)
    join(0, 1)
    weigh(1)
    finish(1, 0)
    finish(1, 1)
    hid_forward(2, 0)
    hid_forward(2, 1)
    gate_up(3, 0)
    gate_up(3, 1)
    wait_chunk(4)
    select(4)
    join(1, 0)
    join(1, 1)
    reduce(0, 0)
    reduce(0, 1)
    weigh(2)
    finish(2, 0)
    finish(2, 1)
    gate_up(4, 0)
    gate_up(4, 1)
    hid_forward(3, 0)
    hid_forward(3, 1)
    join(2, 0)
    join(2, 1)
    reduce(1, 0)
    reduce(1, 1)
    weigh(3)
    finish(3, 0)
    finish(3, 1)
    hid_forward(4, 0)
    hid_forward(4, 1)
    join(3, 0)
    join(3, 1)
    reduce(2, 0)
    reduce(2, 1)
    weigh(4)
    finish(4, 0)
    finish(4, 1)
    join(4, 0)
    join(4, 1)
    reduce(3, 0)
    reduce(3, 1)
    reduce(4, 0)
    reduce(4, 1)

    for j in range(2):
        out_ref[:, out_cols(x, j)] = last[j, x]
        for d in (1, 3, 2):
            x_copy(d, j).wait_recv()
            out_ref[:, out_cols(plus(x, RING - d), j)] = x_in[d - 1, j]

    for n in range(sent[0]):
        remote(blocks.at[0], blocks.at[0], blk_send.at[n], blk_recv.at[0], sibling).wait_send()
    select_send(4).wait_send()
    for i in range(5):
        meta_send(i).wait_send()
        for n in range(6):
            hid_copy(i, x, 0, 1, n).wait_send()
    for j in range(2):
        part_send(4, j).wait_send()
        for d in (1, 3, 2):
            b_copy(4, d, j).wait_send()
            b_copy(3, d, j).wait_send()
            a_copy(d - 1, j).wait_send()
            x_copy(d, j).wait_send()


def per_device(tokens, expert_ids, gate_weights, w_gate, w_up, w_down):
    rows, width = tokens.shape
    ff = w_gate.shape[2]
    cols = w_down.shape[2]
    half = cols // 2
    dma = pltpu.SemaphoreType.DMA
    vmem = pltpu.VMEM
    return pl.pallas_call(
        kernel,
        out_shape=jax.ShapeDtypeStruct((rows, width), BF16),
        in_specs=[
            pl.BlockSpec(memory_space=pl.ANY),
            pl.BlockSpec(memory_space=pltpu.VMEM),
            pl.BlockSpec(memory_space=pltpu.VMEM),
            pl.BlockSpec(memory_space=pl.ANY),
            pl.BlockSpec(memory_space=pl.ANY),
            pl.BlockSpec(memory_space=pl.ANY),
        ],
        out_specs=pl.BlockSpec(memory_space=pltpu.VMEM),
        scratch_shapes=[
            vmem((width, ff), BF16),
            vmem((width, ff), BF16),
            vmem((RING * ff, cols), BF16),
            vmem((64, TOK, width + META), BF16),
            vmem((256, 256), BF16),
            vmem((2, 256, width), BF16),
            vmem((128, width), BF16),
            vmem((5, 16, TOK, META), BF16),
            vmem((4, RING, 2, 256, 256), BF16),
            vmem((256, 256), BF16),
            vmem((256, 256), BF16),
            vmem((2, RING, RING, TOK, half), BF16),
            vmem((2, RING, RING, TOK, half), BF16),
            vmem((2, 2, RING, RING, TOK, half), BF16),
            vmem((2, 2, RING, RING, TOK, half), BF16),
            vmem((4, 3, 2, RING, TOK, half), BF16),
            vmem((3, 2, RING, TOK, half), BF16),
            vmem((3, 2, RING, TOK, half), BF16),
            vmem((2, RING, TOK, half), BF16),
            vmem((3, 2, TOK, half), BF16),
            dma((4,)),
            dma((64,)),
            dma((64,)),
            dma((5,)),
            dma((5,)),
            dma((5,)),
            dma((5,)),
            dma((30,)),
            dma((40,)),
            dma((10,)),
            dma((10,)),
            dma((30,)),
            dma((30,)),
            dma((6,)),
            dma((6,)),
            dma((6,)),
            dma((6,)),
        ],
        compiler_params=pltpu.CompilerParams(
            collective_id=0, has_side_effects=True, vmem_limit_bytes=63 * 2**20
        ),
        cost_estimate=pl.CostEstimate(flops=24 * 10**9, bytes_accessed=24 * 10**6, transcendentals=10**6),
    )(tokens, expert_ids.T, gate_weights.T, w_gate, w_up, w_down)


def solution(mesh):
    in_specs = (
        P(("group", "lane"), None),
        P(("group", "lane"), None),
        P(("group", "lane"), None),
        P(("group", "lane"), None, None),
        P(("group", "lane"), None, None),
        P(("group", "lane"), None, None),
    )
    out_specs = P(("group", "lane"), None)
    return jax.shard_map(
        per_device, mesh=mesh, in_specs=in_specs, out_specs=out_specs, check_vma=False
    )
```

time: 144 us -> 130 us (0.903)
  Pallas kernels: 142 us -> 128 us
    pallas_call x1, Pallas kernels: 142 us -> 128 us  [per_device(): pl.pallas_call(kernel, out_shape=jax.ShapeDtypeStruct((rows, width), BF16...]
where the time goes in v3:
time: 130 us
  Pallas kernels  128 us (98%)
  local copies, waits for them, and re-layouts  1.64 us (1%)
    pallas_call x1, Pallas kernels, per_device(): pl.pallas_call(kernel, out_shape=jax.ShapeDtypeStruct((rows, width), BF16...  128 us

profile of v3, /device:TPU:1, one launch (start us, length us, event | category | flops | bytes accessed | tf_op | source)
XLA Modules:
  0.0 130.0 jit_solution(1943106283494674405)
XLA Ops:
  0.0 128.4 %shard_map.64 = bf16[16,7168]{1,0:T(8,128)(2,1)} custom-call(bf16[16,7168]{1,0:T(8,128)(2,1)} %tok_hbm.1, s32[8,16]{1,0:T(8,128)} %bitcast.2, f32[8,16]{1,0:T(8,128)} %bitcast.3, bf16[1,7168,512]{2,1,0:T(8,128)(2,1)} %wg_hbm.1, bf16[1,7168,512]{2,1,0:T(8,128)(2,1)} %wu_hbm.1, bf16[1,2048,1792]{2,1,0:T(8,128)(2,1)} %wd_hbm.1), custom_call_target="tpu_custom_call" | custom-call | flops 24000000000 | bytes 24000000 | tf_op jit(solution)/shard_map/pallas_call | solution.py:461
  128.4 1.6 %copy.8 = bf16[16,7168]{1,0:T(8,128)(2,1)} copy(bf16[16,7168]{1,0:T(8,128)(2,1)} %shard_map.64) | data formatting | bytes 458752

commit v4 on v3

--- a/solution.py
+++ b/solution.py
@@ -368,16 +368,16 @@
     forward(12)
     gate_up(1, 0)
     own(15)
+    gate_up(1, 1)
     forward(13)
-    gate_up(1, 1)
-    forward(14)
     wait_chunk(2)
     select(2)
-    forward(15)
     hid_forward(1, 0)
     weigh(0)
+    forward(14)
     loads[3].wait()
     finish(0, 0)
+    forward(15)
     finish(0, 1)
     hid_forward(1, 1)
     gate_up(2, 0)

time: 130 us -> 128 us (0.985)
    pallas_call x1, Pallas kernels: 128 us -> 127 us  [per_device(): pl.pallas_call(kernel, out_shape=jax.ShapeDtypeStruct((rows, width), BF16...]
where the time goes in v4:
time: 128 us
  Pallas kernels  127 us (99%)
  local copies, waits for them, and re-layouts  1.64 us (1%)
    pallas_call x1, Pallas kernels, per_device(): pl.pallas_call(kernel, out_shape=jax.ShapeDtypeStruct((rows, width), BF16...  127 us

profile of v4, /device:TPU:1, one launch (start us, length us, event | category | flops | bytes accessed | tf_op | source)
XLA Modules:
  0.0 128.2 jit_solution(7158058615645880889)
XLA Ops:
  0.0 126.6 %shard_map.64 = bf16[16,7168]{1,0:T(8,128)(2,1)} custom-call(bf16[16,7168]{1,0:T(8,128)(2,1)} %tok_hbm.1, s32[8,16]{1,0:T(8,128)} %bitcast.2, f32[8,16]{1,0:T(8,128)} %bitcast.3, bf16[1,7168,512]{2,1,0:T(8,128)(2,1)} %wg_hbm.1, bf16[1,7168,512]{2,1,0:T(8,128)(2,1)} %wu_hbm.1, bf16[1,2048,1792]{2,1,0:T(8,128)(2,1)} %wd_hbm.1), custom_call_target="tpu_custom_call" | custom-call | flops 24000000000 | bytes 24000000 | tf_op jit(solution)/shard_map/pallas_call | solution.py:461
  126.6 1.6 %copy.8 = bf16[16,7168]{1,0:T(8,128)(2,1)} copy(bf16[16,7168]{1,0:T(8,128)(2,1)} %shard_map.64) | data formatting | bytes 458752
